TPU v7x, 32 devices: a whole 2x2x4 slice. The times are simulated.
32 devices in a mesh: paths: 2 (over x), trades: 8 (over z, y), quad: 2 (over core).
Axes of the slice: x: 2, y: 2, z: 4, core: 2. Of those that a mesh axis runs over, the one named last changes fastest.
Arguments:
- factor_paths: bfloat16 [8192, 4, 256], P(('trades', 'quad'), None, 'paths'), parts along dimension 2, may hold values from -6 to 6
- loadings: bfloat16 [16384, 64], P(('trades', 'quad')), may hold values from -0.75 to 0.75
- coeffs: bfloat16 [16384, 64], P(('trades', 'quad')), may hold values from -0.09375 to 0.09375
- trade_blocks: int32 [16384, 4], P(('trades', 'quad')), may hold values from 0 to 511, all different within a row; in each aligned block of 1024 rows (0 to 1023, 1024 to 2047, ...) at most 16 rows name the same one
- trade_set: int32 [16384], P(('trades', 'quad')), may hold values from 0 to 383
- set_order: int32 [384], replicated, may hold values from 0 to 383, each once
- owner_counts: int32 [16], replicated, may hold values from 1 to 32, 384 in all
Outputs:
- exposure: float32 [512, 4, 256], P(('trades', 'quad'), None, 'paths'), parts along dimension 2
There are 2 independent parts, one for each index of `paths`. A program takes and returns all parts, laid end to end along the dimension named above; an argument that names none is the same for every part. Nothing has to cross between parts.
Inputs may be any that keep to these rules, and one draw needn't show every extreme that they name: `trade_blocks`: the 4 blocks of a trade are different; among the trades of one device (aligned blocks of 1024 rows) no block is named by more than 16 trades, and some block by exactly 16. `set_order`: each rank occurs once. `owner_counts`: they sum to 384; some device owns exactly 32.
All inputs are finite; a program needn't handle non-finite values.
Results may differ from a plain program's by a relative error of at most 0.0023.
Values may be sent and summed in bfloat16 or wider, within the bound.
A program may use at most 128 MiB of HBM per device.

v0:
```python
import jax
import jax.numpy as jnp
from jax import lax
from jax.sharding import PartitionSpec as P

FACTORS = 8192
BLOCK_LEN = 16
REFS = 4
HIT_CAP = 16
BASIS = 64
SET_CAP = 32


def chebyshev_sum(under, coef):
    zval = jnp.tanh(under)
    acc = coef[:, 0:1] + coef[:, 1:2] * zval
    before = jnp.ones_like(zval)
    current = zval
    for order in range(2, BASIS):
        after = 2.0 * zval * current - before
        acc = acc + coef[:, order : order + 1] * after
        before = current
        current = after
    return acc


def slot_tables(loadings, trade_blocks):
    local_trades = trade_blocks.shape[0]
    blocks_all = FACTORS // BLOCK_LEN
    pairs = local_trades * REFS
    pair_block = trade_blocks.reshape(pairs)
    order = jnp.argsort(pair_block, stable=True)
    sorted_block = jnp.take(pair_block, order)
    counts = jax.ops.segment_sum(jnp.ones((pairs,), jnp.int32), pair_block, num_segments=blocks_all)
    first = jnp.cumsum(counts) - counts
    slot = jnp.arange(pairs, dtype=jnp.int32) - jnp.take(first, sorted_block)
    position = sorted_block * HIT_CAP + slot
    slot_pair = (
        jnp.full((blocks_all * HIT_CAP,), pairs, jnp.int32).at[position].set(order, mode="drop")
    )
    pair_weights = jnp.concatenate(
        [loadings.reshape(pairs, BLOCK_LEN), jnp.zeros((1, BLOCK_LEN), loadings.dtype)], axis=0
    )
    slot_weights = jnp.take(pair_weights, slot_pair, axis=0).reshape(blocks_all, HIT_CAP, BLOCK_LEN)
    slot_trade = slot_pair // REFS
    return (slot_weights, slot_trade)


def select_rows(total, flat, start, slot_weights):
    count = flat.shape[0]
    width = flat.shape[1]
    nblocks = count // BLOCK_LEN
    first_block = start // BLOCK_LEN
    blocks_data = flat.reshape(nblocks, BLOCK_LEN, width)
    weights = lax.dynamic_slice_in_dim(slot_weights, first_block, nblocks, 0)
    contrib = jnp.einsum("bhi,biw->bhw", weights, blocks_data, preferred_element_type=jnp.float32)
    return lax.dynamic_update_slice_in_dim(total, contrib, first_block, 0)


def on_device(factor_paths, loadings, coeffs, trade_blocks, trade_set, set_order, owner_counts):
    dates = factor_paths.shape[1]
    paths = factor_paths.shape[2]
    width = dates * paths
    local_trades = loadings.shape[0]
    blocks_all = FACTORS // BLOCK_LEN
    owners = lax.axis_size("trades") * lax.axis_size("quad")
    slot_weights, slot_trade = slot_tables(loadings, trade_blocks)
    empty = jnp.zeros((blocks_all, HIT_CAP, width), jnp.float32)
    total = empty
    piece = lax.all_gather(factor_paths, ("trades", "quad"), axis=0, tiled=True)
    count = piece.shape[0]
    flat = piece.reshape(count, width)

    def inner(carry, number):
        part = lax.dynamic_slice_in_dim(flat, number * 256, 256, 0)
        return (select_rows(carry, part, number * 256, slot_weights), None)

    total, _ = lax.scan(inner, total, jnp.arange(count // 256, dtype=jnp.int32))
    under = jax.ops.segment_sum(
        total.reshape(blocks_all * HIT_CAP, width), slot_trade, num_segments=local_trades
    )
    mtm = chebyshev_sum(under, coeffs.astype(jnp.float32))
    ends = jnp.cumsum(owner_counts)
    starts = ends - owner_counts
    rank = jnp.take(set_order, trade_set)
    owner = jnp.sum((ends[None, :] <= rank[:, None]).astype(jnp.int32), axis=1)
    row_of = owner * SET_CAP + rank - jnp.take(starts, owner)
    partial_table = jax.ops.segment_sum(mtm, row_of, num_segments=owners * SET_CAP)
    netted = lax.psum_scatter(partial_table, ("trades", "quad"), scatter_dimension=0, tiled=True)
    return jnp.maximum(netted, 0.0).reshape(SET_CAP, dates, paths)


def solution(mesh):
    in_specs = (
        P(("trades", "quad"), None, "paths"),
        P(("trades", "quad"), None),
        P(("trades", "quad"), None),
        P(("trades", "quad"), None),
        P(("trades", "quad")),
        P(),
        P(),
    )
    out_specs = P(("trades", "quad"), None, "paths")
    return jax.shard_map(
        on_device, mesh=mesh, in_specs=in_specs, out_specs=out_specs, check_vma=False
    )
```

profile of v0, /device:TPU:0, one launch (start us, length us, event | category | flops | bytes accessed | tf_op | source)
XLA Modules:
  0.0 455.1 jit_solution(10387620417919792176)
XLA Ops:
  8.5 5.8 %sort.17 = (s32[4096]{0:T(1024)}, s32[4096]{0:T(1024)S(1)}) sort(s32[4096]{0:T(1024)S(1)} %reshape.124, s32[4096]{0:T(1024)S(1)} %iota.10), dimensions={0}, to_apply=%region_2.3 | sort | flops 49152 | bytes 65536 | tf_op jit(solution)/shard_map/jit(argsort)/sort | solution.py:32
  14.3 23.0 %gather_fusion.1 = s32[4096]{0:T(1024)S(1)} fusion(s32[4096]{0:T(1024)S(1)} %reshape.124, s32[4096]{0:T(1024)S(1)} %fusion.113), kind=kCustom, calls=%fused_computation.1 | custom fusion | bytes 49152 | tf_op jit(solution)/shard_map/jit(_take)/gather | solution.py:33
  37.4 28.8 %scatter_custom_fusion = s32[512]{0:T(512)S(1)} fusion(s32[4096]{0:T(1024)S(1)} %reshape.124, s32[4096]{0:T(1024)S(1)} %broadcast.126, s32[]{:T(128)} %constant.150.clone.1), kind=kCustom, calls=%fused_computation.206 | custom fusion | flops 4096 | bytes 2052 | tf_op jit(solution)/shard_map/scatter-add | solution.py:34
  67.4 25.8 %gather_fusion.2 = s32[4096]{0:T(1024)S(1)} fusion(s32[512]{0:T(512)S(1)} %bitcast_subtract_fusion, s32[4096]{0:T(1024)S(1)} %fusion.112), kind=kCustom, calls=%fused_computation.2 | custom fusion | bytes 49152 | tf_op jit(solution)/shard_map/jit(_take)/gather | solution.py:36
  93.3 15.7 %scatter_custom_fusion.1 = s32[8192]{0:T(1024)S(1)} fusion(s32[4096]{0:T(1024)S(1)} %compare_select_fusion, s32[4096]{0:T(1024)S(1)} %get-tuple-element.72, s32[]{:T(128)} %constant.157.clone.1), kind=kCustom, calls=%fused_computation.178 | custom fusion | bytes 32772 | tf_op jit(solution)/shard_map/scatter | solution.py:39
  109.7 24.0 %gather_fusion.3 = bf16[8192,16]{1,0:T(8,128)(2,1)S(1)} fusion(bf16[4097,16]{1,0:T(8,128)(2,1)S(1)} %concatenate.3, s32[8192]{0:T(1024)S(1)} %get-tuple-element.162), kind=kCustom, calls=%fused_computation.3 | custom fusion | bytes 557056 | tf_op jit(solution)/shard_map/jit(_take)/gather | solution.py:44
  133.8 6.9 %gather_fusion = s32[1024]{0:T(1024)S(1)} fusion(s32[384]{0:T(512)S(1)} %copy-done, s32[1024]{0:T(1024)S(1)} %fusion.115), kind=kCustom, calls=%fused_computation | custom fusion | bytes 12288 | tf_op jit(solution)/shard_map/jit(_take)/gather | solution.py:85
  141.5 4.4 compare_select_fusion.4
  146.0 5.6 %fusion.114 = s32[1024]{0:T(1024)S(1)} fusion(pred[1024]{0:T(1024)(128)(4,1)S(1)} %get-tuple-element.82, pred[1024]{0:T(1024)(128)(4,1)S(1)} %get-tuple-element.81, pred[1024]{0:T(1024)(128)(4,1)S(1)} %get-tuple-element.80, pred[1024]{0:T(1024)(128)(4,1)S(1)} %get-tuple-element.79, pred[1024]{0:T(1024)(128)(4,1)S(1)} %get-tuple-element.78, ...), kind=kLoop, calls=%fused_computation.201 | loop fusion | flops 19456 | bytes 25636 | tf_op jit(solution)/shard_map/sub | solution.py:87
  151.9 4.7 %broadcast_select_fusion = bf16[512,16,16]{2,1,0:T(8,128)(2,1)} fusion(bf16[512,16,16]{2,1,0:T(8,128)(2,1)S(1)} %bitcast.104, pred[512,16]{1,0:T(8,128)(4,1)S(1)} %broadcast_in_dim.78), kind=kLoop, calls=%fused_computation.136 | loop fusion | flops 131072 | bytes 532480 | tf_op jit(solution)/shard_map/jit(_take)/select_n | solution.py:44
  156.6 8.0 %copy.21 = bf16[1024,8,4,128]{3,1,2,0:T(8,128)(2,1)} copy(bf16[1024,8,4,128]{3,2,1,0:T(4,128)(2,1)} %bitcast.105) | data formatting | bytes 16777216
  164.6 7.9 %broadcast_in_dim.77 = f32[512,16,512]{2,1,0:T(8,128)} broadcast(f32[]{:T(128)} %constant.149.clone.1), dimensions={} | broadcast | bytes 16777220 | tf_op jit(solution)/shard_map/broadcast_in_dim | solution.py:68
  172.5 130.9 %while.12 = (s32[]{:T(128)}, f32[512,16,512]{2,1,0:T(8,128)}, s32[32]{0:T(128)S(1)}, bf16[512,16,16]{2,1,0:T(8,128)(2,1)}, bf16[8192,512]{1,0:T(8,128)(2,1)}, /*...) while((s32[]{:T(128)}, f32[512,16,512]{2,1,0:T(8,128)}, ...), condition=%wide.region_8.9_spmd, body=%wide.region_7.8_spmd.sunk | while | flops 4194327 | bytes 1377642 | solution.py:78
  182.9 1.9 convolution_dynamic-update-slice_fusion.2
  211.5 1.9 convolution_dynamic-update-slice_fusion.2
  240.1 1.9 convolution_dynamic-update-slice_fusion.2
  244.2 1.9 convolution_dynamic-update-slice_fusion.2
  256.5 1.9 convolution_dynamic-update-slice_fusion.2
  272.9 1.9 convolution_dynamic-update-slice_fusion.2
  277.0 1.9 convolution_dynamic-update-slice_fusion.2
  303.4 49.8 %scatter_custom_fusion.2 = f32[1024,512]{1,0:T(8,128)S(1)} fusion(s32[8192]{0:T(1024)S(1)} %get-tuple-element.163, f32[8192,512]{1,0:T(8,128)} %bitcast.102, f32[]{:T(128)} %constant.149.clone.1), kind=kCustom, calls=%fused_computation.158 | custom fusion | flops 4194304 | bytes 2097664 | tf_op jit(solution)/shard_map/scatter-add | solution.py:79
  353.2 16.5 %multiply_add_fusion = (f32[1024,512]{1,0:T(8,128)}, f32[1024,512]{1,0:T(8,128)}, f32[1024,512]{1,0:T(8,128)}) fusion(f32[1024,512]{1,0:T(8,128)S(1)} %scatter_custom_fusion.2, f32[1024]{0:T(1024)S(1)} %bitcast.134, f32[1024]{0:T(1024)S(1)} %bitcast.133, f32[1024]{0:T(1024)S(1)} %bitcast.132, f32[1024]{0:T(1024)S(1)} %bitcast.131, f32[1024]{0:T(1024)S(1)} %bitcast.130, ...), kind=kLoop, calls=%fused_computation.93 | loop fusion | flops 89653248 | bytes 8568832 | tf_op jit(solution)/shard_map/add | solution.py:21
  369.7 16.7 %scatter_custom_fusion.3 = f32[512,512]{1,0:T(8,128)} fusion(s32[1024]{0:T(1024)S(1)} %fusion.114, f32[1024,512]{1,0:T(8,128)} %get-tuple-element.93, f32[1024]{0:T(1024)S(1)} %bitcast.108, f32[1024]{0:T(1024)S(1)} %bitcast.127, f32[1024]{0:T(1024)S(1)} %bitcast.126, f32[1024]{0:T(1024)S(1)} %bitcast.125, f32[1024]{0:T(1024)S(1)} %bitcast.124, ...), kind=kCustom, calls=%fused_computation.13 | custom fusion | flops 58720256 | bytes 9519112 | tf_op jit(solution)/shard_map/scatter-add | solution.py:88
  386.4 60.3 %reduce-scatter.2.cloned.1.call-done = f32[32,512]{1,0:T(8,128)} async-done(((f32[512,512]{1,0:T(8,128)}), f32[32,512]{1,0:T(8,128)}) %reduce-scatter.2.cloned.1.call-update) | async-done | bytes 65552 | tf_op jit(solution)/shard_map/reduce_scatter | solution.py:89
  (138 shorter events, 102.3 us)
Async XLA Ops:
  6.5 127.2 %copy-start = (s32[384]{0:T(512)S(1)}, s32[384]{0:T(512)}, u32[]{:S(2)}) copy-start(s32[384]{0:T(512)} %param.14) | copy-start | bytes 4612
  6.5 150.0 %all-gather.2.cloned.1.call-start = ((), (), s32[]{:S(2)}) async-start(), calls=%async_computation.1 | async-start | bytes 8912896 | tf_op jit(solution)/shard_map/all_gather | solution.py:70
  7.3 439.5 %reduce-scatter.2.cloned.1.call-start = ((), (), s32[]{:S(2)}) async-start(), calls=%async_computation.2 | async-start | bytes 1114112 | tf_op jit(solution)/shard_map/reduce_scatter | solution.py:89
  14.3 52.3 %copy-start.2 = (bf16[1024,64]{0,1:T(8,128)(2,1)S(1)}, bf16[1024,64]{0,1:T(8,128)(2,1)}, u32[]{:S(2)}) copy-start(bf16[1024,64]{0,1:T(8,128)(2,1)} %param.10) | copy-start | bytes 393220
  67.4 41.8 %copy-start.4 = (s32[16]{0:T(128)S(1)}, s32[16]{0:T(128)}, u32[]{:S(2)}) copy-start(s32[16]{0:T(128)} %param.15) | copy-start | bytes 196
  109.7 24.1 %copy-start.3 = (s32[1024]{0:T(1024)S(1)}, s32[1024]{0:T(1024)}, u32[]{:S(2)}) copy-start(s32[1024]{0:T(1024)} %param.13) | copy-start | bytes 12292
  133.8 17.8 %copy-start.1 = (bf16[1024,64]{0,1:T(8,128)(2,1)S(1)}, bf16[1024,64]{0,1:T(8,128)(2,1)}, u32[]{:S(2)}) copy-start(bf16[1024,64]{0,1:T(8,128)(2,1)} %param.11) | copy-start | bytes 393220
Sparse Core Ops, SparseCore 0:
  9.5 77.5 all-gather.1
  386.6 60.1 reduce-scatter.1
where the time goes:
time: 458 us; the launch traced here: 455 us
  local copies, waits for them, and re-layouts  165 us (36%)
  other arithmetic  134 us (29%)
  waiting for transfers between devices  61 us (13%)
  matrix products  59.3 us (13%)
  loops' own time  21.9 us (5%)
  between operations  13.7 us (3%)
    reduce_scatter x1, waiting for transfers between devices, on_device(): lax.psum_scatter(partial_table, ('trades', 'quad'), scatter_dimension=0,...  60.3 us
    dot_general x32, matrix products, select_rows(): jnp.einsum('bhi,biw->bhw', weights, blocks_data, preferred_element_type=j...  59.3 us
    scatter-add x1, other arithmetic, on_device(): jax.ops.segment_sum(total.reshape(blocks_all * HIT_CAP, width), slot_trad...  49.8 us
    dynamic_slice x32, local copies, waits for them, and re-layouts, inner(): part = lax.dynamic_slice_in_dim(flat, number * 256, 256, 0)  31.1 us
    scatter-add x1, other arithmetic, slot_tables(): jax.ops.segment_sum(jnp.ones((pairs,), jnp.int32), pair_block, num_segmen...  28.8 us
    gather x1, local copies, waits for them, and re-layouts, slot_tables(): slot = jnp.arange(pairs, dtype=jnp.int32) - jnp.take(first, sorted_block)  25.8 us
    gather x1, local copies, waits for them, and re-layouts, slot_tables(): jnp.take(pair_weights, slot_pair, axis=0)  24 us
    gather x1, local copies, waits for them, and re-layouts, slot_tables(): sorted_block = jnp.take(pair_block, order)  23 us
  transfers between devices with their start and end apart: 2, of which 1 were waited for; matrix products, arithmetic and copies ran while one was open for 33% of the time, Pallas kernels for 0%

commit v1 on v0

v1 whole, which is shorter than its diff:
```python
import functools

import jax
import jax.numpy as jnp
import numpy as np
from jax import lax
from jax.experimental import pallas as pl
from jax.experimental.pallas import tpu as pltpu
from jax.sharding import PartitionSpec as P

BLOCK_LEN = 16
REFS = 4
SET_CAP = 32
STEP = 8
MESH = pl.DeviceIdType.MESH


def two_level(basis):
    now = np.eye(basis, dtype=np.float32)
    out = np.zeros((basis, basis), np.float32)
    for a in range(basis // STEP - 1, 0, -1):
        out[a * STEP] = now[a * STEP]
        for b in range(1, STEP):
            out[a * STEP + b] = 2 * now[a * STEP + b]
            now[a * STEP - b] -= now[a * STEP + b]
    out[:STEP] = now[:STEP]
    return out


def kernel(trades, fx, load, coef, blocks, tset, order, counts, mix, out,
           gath, weight, spread, acc, ct, zt, mtm, net, tab, got1, sum1, got2, sum2, got3,
           sz, rz, sy, ry, ss, rs, s1, r1, s2, r2, s3, r3):
    dates, nloc, paths = fx.shape
    local = load.shape[0]
    basis = coef.shape[1]
    half = trades // 2
    owners = trades * 2
    nsets = order.shape[1]
    rows = owners * SET_CAP
    factors = owners * nloc

    t = lax.axis_index("trades")
    c = lax.axis_index("quad")
    hi, lo = t // 2, lax.rem(t, 2)
    sib = {"trades": t, "quad": 1 - c}
    across = {"trades": hi * 2 + (1 - lo), "quad": c}

    def zpos(k):
        return lax.rem(hi + k, half)

    def zdev(k):
        return {"trades": zpos(k) * 2 + lo, "quad": c}

    def shard(h, l, q):
        return (h * 2 + l) * 2 + q

    me = shard(hi, lo, c)

    barrier = pltpu.get_barrier_semaphore()
    for dev in [sib, across] + [zdev(k) for k in range(1, half)]:
        pl.semaphore_signal(barrier, inc=1, device_id=dev, device_id_type=MESH)
    pl.semaphore_wait(barrier, half + 1)

    def rcopy(src, dst, ssem, rsem, dev):
        return pltpu.make_async_remote_copy(
            src_ref=src, dst_ref=dst, send_sem=ssem, recv_sem=rsem,
            device_id=dev, device_id_type=MESH)

    pending = []

    def send(*args):
        cp = rcopy(*args)
        cp.start()
        pending.append(cp)

    def own(d):
        src, dst = fx.at[d], gath.at[d, me]
        for k in range(1, half):
            send(src, dst, sz.at[d, k - 1], rz.at[d, k - 1], zdev(k))
        send(src, dst, sy.at[d, 0], ry.at[d, 0], across)
        send(src, dst, ss.at[d, 0], rs.at[d, 0], sib)

    def arrive_z(d, k):
        slot = gath.at[d, shard(zpos(half - k), lo, c)]
        rcopy(slot, slot, sz.at[d, k - 1], rz.at[d, k - 1], zdev(k)).wait_recv()
        send(slot, slot, sy.at[d, k], ry.at[d, k], across)
        send(slot, slot, ss.at[d, k], rs.at[d, k], sib)

    def arrive_y(d, k):
        slot = gath.at[d, shard(zpos(half - k), 1 - lo, c)]
        rcopy(slot, slot, sy.at[d, k], ry.at[d, k], across).wait_recv()
        send(slot, slot, ss.at[d, half + k], rs.at[d, half + k], sib)

    def arrive_s(d):
        for k in range(half):
            slot = gath.at[d, shard(zpos(half - k), lo, 1 - c)]
            rcopy(slot, slot, ss.at[d, k], rs.at[d, k], sib).wait_recv()
        for k in range(half):
            slot = gath.at[d, shard(zpos(half - k), 1 - lo, 1 - c)]
            rcopy(slot, slot, ss.at[d, half + k], rs.at[d, half + k], sib).wait_recv()

    own(0)
    own(1)

    for d in range(dates):
        gath[d, me] = fx[d]

    ct[...] = lax.dot_general(mix[...], coef[...], (((1,), (1,)), ((), ())),
                              preferred_element_type=jnp.float32)

    j = lax.broadcasted_iota(jnp.int32, (REFS * BLOCK_LEN, 128), 0)
    l = lax.broadcasted_iota(jnp.int32, (REFS * BLOCK_LEN, 128), 1)
    for r in range(REFS):
        pick = jnp.where(j == r * BLOCK_LEN + (l & (BLOCK_LEN - 1)), 1.0, 0.0).astype(jnp.bfloat16)
        spread[r] = jnp.dot(load[...], pick, preferred_element_type=jnp.float32)

    def build(first, count):
        @pl.loop(first, first + count)
        def _(i):
            at = pl.ds(pl.multiple_of(i * 16, 16), 16)
            ids = blocks[at, :]
            lane = lax.broadcasted_iota(jnp.int32, (16, 128), 1) // BLOCK_LEN
            diff = [ids[:, r:r + 1] - lane for r in range(REFS)]
            val = [spread[r, at, :] for r in range(REFS)]
            for n in range(factors // 128):
                v = jnp.zeros((16, 128), jnp.float32)
                for r in range(REFS):
                    v = jnp.where(diff[r] == n * (128 // BLOCK_LEN), val[r], v)
                weight[at, n * 128:(n + 1) * 128] = v.astype(jnp.bfloat16)

    pieces = half
    each = local // 16 // pieces
    for k in range(pieces):
        build(k * each, each)
        if k + 1 < half:
            arrive_z(0, k + 1)

    d0 = lax.broadcasted_iota(jnp.int32, (owners, owners), 0)
    d1 = lax.broadcasted_iota(jnp.int32, (owners, owners), 1)
    cnt = jnp.broadcast_to(counts[...], (owners, owners))
    starts = jnp.sum(jnp.where(d1 < d0, cnt, 0), axis=1, keepdims=True)
    ends = jnp.sum(jnp.where(d1 <= d0, cnt, 0), axis=1, keepdims=True)
    rank = jnp.broadcast_to(order[...], (owners, nsets))
    od = lax.broadcasted_iota(jnp.int32, (owners, nsets), 0)
    place = ((od & 1) * 2 + ((od >> 1) & 1)) * half + (od >> 2)
    mine = (starts <= rank) & (rank < ends)
    where_owner = jnp.sum(jnp.where(mine, place, 0), axis=0, keepdims=True)
    where_slot = jnp.sum(jnp.where(mine, rank - starts, 0), axis=0, keepdims=True)
    sid = lax.broadcasted_iota(jnp.int32, (nsets, local), 0)
    hot = jnp.where(sid == tset[...], 1.0, 0.0).astype(jnp.bfloat16)
    both = jnp.concatenate(
        [jnp.broadcast_to(where_owner, (8, nsets)), jnp.broadcast_to(where_slot, (8, nsets))], axis=0)
    found = jnp.dot(both.astype(jnp.float32).astype(jnp.bfloat16), hot,
                    preferred_element_type=jnp.float32)
    row = (found[0:1, :] * SET_CAP + found[8:9, :]).astype(jnp.int32)
    rid = lax.broadcasted_iota(jnp.int32, (rows, local), 0)
    net[...] = jnp.where(rid == row, 1.0, 0.0).astype(jnp.bfloat16)

    for k in range(half):
        arrive_y(0, k)
    arrive_s(0)

    per = 2048 // nloc

    def multiply(d):
        acc[...] = jnp.zeros_like(acc)

        @pl.loop(0, owners // per)
        def _(i):
            cols = pl.ds(pl.multiple_of(i * (per * nloc), 128), per * nloc)
            part = gath[d, pl.ds(i * per, per)].reshape(per * nloc, paths)
            acc[...] += jnp.dot(weight[:, cols], part, preferred_element_type=jnp.float32)

    def price():
        @pl.loop(0, local // 128)
        def _(i):
            at = pl.ds(pl.multiple_of(i * 128, 128), 128)
            zt[...] = jnp.tanh(acc[at, :].T)
            for p in range(paths // 32):
                z = zt[p * 32:(p + 1) * 32, :]
                z2 = z + z
                tk = [None, z]
                for b in range(2, STEP + 1):
                    tk.append(z2 * tk[b - 1] - (1.0 if b == 2 else tk[b - 2]))
                y = tk[STEP]
                y2 = y + y
                b1 = b2 = None
                for a in range(basis // STEP - 1, -1, -1):
                    q = jnp.broadcast_to(ct[a * STEP:a * STEP + 1, at], z.shape)
                    for b in range(1, STEP):
                        q = q + ct[a * STEP + b:a * STEP + b + 1, at] * tk[b]
                    if b1 is None:
                        new = q
                    elif b2 is None:
                        new = q + (y if a == 0 else y2) * b1
                    else:
                        new = q + ((y if a == 0 else y2) * b1 - b2)
                    b1, b2 = new, b1
                high = b1.astype(jnp.bfloat16)
                mtm[p * 32:(p + 1) * 32, at] = high
                mtm[paths + p * 32:paths + (p + 1) * 32, at] = (
                    b1 - high.astype(jnp.float32)).astype(jnp.bfloat16)

    h1, h2 = rows // 2, rows // 4

    def netting(d):
        full = lax.dot_general(net[...], mtm[...], (((1,), (1,)), ((), ())),
                               preferred_element_type=jnp.float32)
        tab[d] = full[:, :paths] + full[:, paths:]
        away = pl.multiple_of((1 - c) * h1, h1)
        send(tab.at[d, pl.ds(away, h1)], got1.at[d], s1.at[d], r1.at[d], sib)

    def stage2(d):
        rcopy(got1.at[d], got1.at[d], s1.at[d], r1.at[d], sib).wait_recv()
        sum1[d] = tab[d, pl.ds(pl.multiple_of(c * h1, h1), h1)] + got1[d]
        away = pl.multiple_of((1 - lo) * h2, h2)
        send(sum1.at[d, pl.ds(away, h2)], got2.at[d], s2.at[d], r2.at[d], across)

    def stage3(d):
        rcopy(got2.at[d], got2.at[d], s2.at[d], r2.at[d], across).wait_recv()
        sum2[d] = sum1[d, pl.ds(pl.multiple_of(lo * h2, h2), h2)] + got2[d]
        for k in range(1, half):
            src = sum2.at[d, pl.ds(pl.multiple_of(zpos(k) * SET_CAP, SET_CAP), SET_CAP)]
            send(src, got3.at[d, k - 1], s3.at[d, k - 1], r3.at[d, k - 1], zdev(k))

    def finish(d):
        total = sum2[d, pl.ds(pl.multiple_of(hi * SET_CAP, SET_CAP), SET_CAP)]
        for k in range(1, half):
            slot = got3.at[d, k - 1]
            rcopy(slot, slot, s3.at[d, k - 1], r3.at[d, k - 1], zdev(k)).wait_recv()
            total = total + got3[d, k - 1]
        out[d] = jnp.maximum(total, 0.0)

    for d in range(dates):
        if d + 2 < dates:
            own(d + 2)
        multiply(d)
        if d + 1 < dates:
            for k in range(1, half):
                arrive_z(d + 1, k)
        price()
        netting(d)
        if d + 1 < dates:
            for k in range(half):
                arrive_y(d + 1, k)
        stage2(d)
        stage3(d)
        if d + 1 < dates:
            arrive_s(d + 1)
    for d in range(dates):
        finish(d)
    for cp in pending:
        cp.wait_send()


def on_device(trades, factor_paths, loadings, coeffs, trade_blocks, trade_set, set_order, owner_counts):
    nloc, dates, paths = factor_paths.shape
    local = loadings.shape[0]
    basis = coeffs.shape[1]
    owners = 2 * trades
    half = trades // 2
    rows = owners * SET_CAP
    dma = pltpu.SemaphoreType.DMA
    fx = jnp.transpose(factor_paths, (1, 0, 2))
    f32, bf16 = jnp.float32, jnp.bfloat16
    result = pl.pallas_call(
        functools.partial(kernel, trades),
        out_shape=jax.ShapeDtypeStruct((dates, SET_CAP, paths), f32),
        in_specs=[pl.BlockSpec(memory_space=pltpu.VMEM)] * 8,
        out_specs=pl.BlockSpec(memory_space=pltpu.VMEM),
        scratch_shapes=[
            pltpu.VMEM((dates, owners, nloc, paths), bf16),
            pltpu.VMEM((local, owners * nloc), bf16),
            pltpu.VMEM((REFS, local, 128), f32),
            pltpu.VMEM((local, paths), f32),
            pltpu.VMEM((basis, local), f32),
            pltpu.VMEM((paths, 128), f32),
            pltpu.VMEM((2 * paths, local), bf16),
            pltpu.VMEM((rows, local), bf16),
            pltpu.VMEM((dates, rows, paths), f32),
            pltpu.VMEM((dates, rows // 2, paths), f32),
            pltpu.VMEM((dates, rows // 2, paths), f32),
            pltpu.VMEM((dates, rows // 4, paths), f32),
            pltpu.VMEM((dates, rows // 4, paths), f32),
            pltpu.VMEM((dates, half - 1, SET_CAP, paths), f32),
            dma((dates, half - 1)), dma((dates, half - 1)),
            dma((dates, half)), dma((dates, half)),
            dma((dates, 2 * half)), dma((dates, 2 * half)),
            dma((dates,)), dma((dates,)),
            dma((dates,)), dma((dates,)),
            dma((dates, half - 1)), dma((dates, half - 1)),
        ],
        compiler_params=pltpu.CompilerParams(
            collective_id=0, has_side_effects=True, vmem_limit_bytes=56 * 1024 * 1024
        ),
    )(
        fx, loadings, coeffs, trade_blocks, trade_set.reshape(1, -1),
        set_order.reshape(1, -1), owner_counts.reshape(1, -1),
        jnp.asarray(two_level(basis), bf16),
    )
    return jnp.transpose(result, (1, 0, 2))


def solution(mesh):
    in_specs = (
        P(("trades", "quad"), None, "paths"),
        P(("trades", "quad"), None),
        P(("trades", "quad"), None),
        P(("trades", "quad"), None),
        P(("trades", "quad")),
        P(),
        P(),
    )
    out_specs = P(("trades", "quad"), None, "paths")
    return jax.shard_map(
        functools.partial(on_device, mesh.shape["trades"]),
        mesh=mesh, in_specs=in_specs, out_specs=out_specs, check_vma=False,
    )
```

time: 458 us -> 116 us (0.25)
  local copies, waits for them, and re-layouts: 165 us -> 8.15 us
  other arithmetic: 134 us -> 0 us
  Pallas kernels: 0 us -> 108 us
  waiting for transfers between devices: 61 us -> 0 us
  matrix products: 59.3 us -> 0 us
  loops' own time: 21.9 us -> 0 us
  between operations: 13.7 us -> 0.01 us
    pallas_call x0 -> x1, Pallas kernels: none -> 108 us  [on_device(): pl.pallas_call(functools.partial(kernel, trades), out_shape=jax.ShapeDtyp...]
    scatter-add x3 -> x0, other arithmetic: 95.3 us -> none  [the longest x1 49.8 us: on_device(): jax.ops.segment_sum(total.reshape(blocks_all * HIT_CAP, width), slot_trad...]
    gather x5 -> x0, local copies, waits for them, and re-layouts: 80.5 us -> none  [the longest x1 25.8 us: slot_tables(): slot = jnp.arange(pairs, dtype=jnp.int32) - jnp.take(first, sorted_block)]
    reduce_scatter x1 -> x0, waiting for transfers between devices: 60.3 us -> none  [on_device(): lax.psum_scatter(partial_table, ('trades', 'quad'), scatter_dimension=0,...]
    dot_general x32 -> x0, matrix products: 59.3 us -> none  [select_rows(): jnp.einsum('bhi,biw->bhw', weights, blocks_data, preferred_element_type=j...]
    dynamic_slice x64 -> x0, local copies, waits for them, and re-layouts: 49.7 us -> none  [the longest x32 31.1 us: inner(): part = lax.dynamic_slice_in_dim(flat, number * 256, 256, 0)]
    another operation x1 -> x0, loops' own time: 21.9 us -> none  [on_device(): total, _ = lax.scan(inner, total, jnp.arange(count // 256, dtype=jnp.int32))]
    add x1 -> x0, other arithmetic: 16.5 us -> none  [chebyshev_sum(): acc = acc + coef[:, order:order + 1] * after]
  transfers between devices with their start and end apart: 2 -> 0, of which waited for: 1 -> 0; matrix products, arithmetic and copies ran while one was open for 33% -> 0% of each run, Pallas kernels for 0% -> 0%
where the time goes in v1:
time: 116 us
  Pallas kernels  108 us (93%)
  local copies, waits for them, and re-layouts  8.15 us (7%)
    pallas_call x1, Pallas kernels, on_device(): pl.pallas_call(functools.partial(kernel, trades), out_shape=jax.ShapeDtyp...  108 us
    unnamed x10, local copies, waits for them, and re-layouts  6.07 us

profile of v1, /device:TPU:0, one launch (start us, length us, event | category | flops | bytes accessed | tf_op | source)
XLA Modules:
  0.0 116.2 jit_solution(5842861455475155915)
XLA Ops:
  0.0 0.0 copy-start.2
  0.0 0.0 copy-start
  0.0 0.7 copy-done.2
  0.7 0.6 reshape.10.order
  1.2 1.7 %copy.10.load = bf16[1024,64]{1,0:T(8,128)(2,1)} copy(bf16[1024,64]{0,1:T(8,128)(2,1)} %param.9) | data formatting | bytes 262144 | tf_op args[1]
  3.0 1.7 %copy.11.coef = bf16[1024,64]{1,0:T(8,128)(2,1)} copy(bf16[1024,64]{0,1:T(8,128)(2,1)} %param.10) | data formatting | bytes 262144 | tf_op args[2]
  4.7 0.0 copy-done
  4.7 0.0 copy-start.1
  4.7 0.9 copy.15
  5.6 0.0 copy-done.1
  5.6 1.0 copy.12.blocks
  6.6 108.1 %shard_map.82 = f32[4,32,128]{2,1,0:T(8,128)} custom-call(bf16[4,512,128]{2,1,0:T(8,128)(2,1)} %bitcast.6, bf16[1024,64]{1,0:T(8,128)(2,1)} %copy.10.load, bf16[1024,64]{1,0:T(8,128)(2,1)} %copy.11.coef, s32[1024,4]{1,0:T(8,128)} %copy.12.blocks, s32[1,1024]{1,0:T(1,128)} %bitcast.8, s32[1,384]{1,0:T(1,128)} %reshape.10.order, s32[1,16]{1,0:T(1,128)} %bitcast.9, ...), custom_call_target="tpu_custom_call" | custom-call | tf_op jit(solution)/shard_map/pallas_call | solution.py:266
  114.7 1.5 %copy.13 = f32[32,4,128]{2,1,0:T(4,128)} copy(f32[32,4,128]{2,0,1:T(8,128)} %bitcast.7) | data formatting | bytes 131072 | tf_op jit(solution)/shard_map/transpose | solution.py:301
Async XLA Ops:
  0.0 0.7 copy-start.2
  0.0 4.7 %copy-start = (bf16[512,4,128]{2,1,0:T(4,128)(2,1)S(1)}, bf16[512,4,128]{2,1,0:T(4,128)(2,1)}, u32[]{:S(2)}) copy-start(bf16[512,4,128]{2,1,0:T(4,128)(2,1)} %param.8) | copy-start | bytes 1572868
  4.7 0.9 copy-start.1

commit v2 on v1

--- a/solution.py
+++ b/solution.py
@@ -73,37 +73,67 @@
         cp.start()
         pending.append(cp)
 
-    def own(d):
-        src, dst = fx.at[d], gath.at[d, me]
-        for k in range(1, half):
-            send(src, dst, sz.at[d, k - 1], rz.at[d, k - 1], zdev(k))
-        send(src, dst, sy.at[d, 0], ry.at[d, 0], across)
-        send(src, dst, ss.at[d, 0], rs.at[d, 0], sib)
+    relayed = half == 4
+    edge = (hi == 0) | (hi == half - 1)
+
+    ks = list(range(1, half, 2)) + list(range(2, half, 2))
+
+    def part_of(d, s):
+        return gath.at[d // 2, s, d % 2]
+
+    def own_near(d):
+        send(fx.at[d], part_of(d, me), sy.at[d, 0], ry.at[d, 0], across)
+        send(fx.at[d], part_of(d, me), ss.at[d, 0], rs.at[d, 0], sib)
+
+    def own_far(d):
+        for k in ks:
+            cp = rcopy(fx.at[d], part_of(d, me), sz.at[d, k - 1], rz.at[d, k - 1], zdev(k))
+            if relayed and k == 2:
+                pl.when(edge)(cp.start)
+            else:
+                cp.start()
+            pending.append(cp)
 
     def arrive_z(d, k):
-        slot = gath.at[d, shard(zpos(half - k), lo, c)]
+        slot = part_of(d, shard(zpos(half - k), lo, c))
         rcopy(slot, slot, sz.at[d, k - 1], rz.at[d, k - 1], zdev(k)).wait_recv()
+        if relayed and k != 2:
+            passer, step = (2, 1) if k == 1 else (1, 3)
+            relay = rcopy(slot, slot, sz.at[d, 1], rz.at[d, 1], zdev(step))
+            pl.when(hi == passer)(relay.start)
         send(slot, slot, sy.at[d, k], ry.at[d, k], across)
         send(slot, slot, ss.at[d, k], rs.at[d, k], sib)
 
     def arrive_y(d, k):
-        slot = gath.at[d, shard(zpos(half - k), 1 - lo, c)]
+        slot = part_of(d, shard(zpos(half - k), 1 - lo, c))
         rcopy(slot, slot, sy.at[d, k], ry.at[d, k], across).wait_recv()
         send(slot, slot, ss.at[d, half + k], rs.at[d, half + k], sib)
 
-    def arrive_s(d):
-        for k in range(half):
-            slot = gath.at[d, shard(zpos(half - k), lo, 1 - c)]
-            rcopy(slot, slot, ss.at[d, k], rs.at[d, k], sib).wait_recv()
-        for k in range(half):
-            slot = gath.at[d, shard(zpos(half - k), 1 - lo, 1 - c)]
-            rcopy(slot, slot, ss.at[d, half + k], rs.at[d, half + k], sib).wait_recv()
-
-    own(0)
-    own(1)
-
+    def multiply(e, k, side):
+        l = lo if side == 0 else 1 - lo
+        n = side * half + k
+        h = zpos(half - k)
+        for d in (2 * e, 2 * e + 1):
+            slot = part_of(d, shard(h, l, 1 - c))
+            rcopy(slot, slot, ss.at[d, n], rs.at[d, n], sib).wait_recv()
+        first = shard(h, l, 0)
+        cols = pl.ds(pl.multiple_of(first * nloc, 2 * nloc), 2 * nloc)
+        part = jnp.concatenate(
+            [jnp.concatenate([gath[e, first + q, 0], gath[e, first + q, 1]], axis=1)
+             for q in range(2)], axis=0)
+        new = jnp.dot(weight[:, cols], part, preferred_element_type=jnp.float32)
+        if n == 0:
+            acc[e] = new
+        else:
+            acc[e] += new
+
+    own_far(0)
     for d in range(dates):
-        gath[d, me] = fx[d]
+        own_near(d)
+    own_far(1)
+
+    for d in range(dates):
+        gath[d // 2, me, d % 2] = fx[d]
 
     ct[...] = lax.dot_general(mix[...], coef[...], (((1,), (1,)), ((), ())),
                               preferred_element_type=jnp.float32)
@@ -128,12 +158,14 @@
                     v = jnp.where(diff[r] == n * (128 // BLOCK_LEN), val[r], v)
                 weight[at, n * 128:(n + 1) * 128] = v.astype(jnp.bfloat16)
 
-    pieces = half
-    each = local // 16 // pieces
-    for k in range(pieces):
-        build(k * each, each)
-        if k + 1 < half:
-            arrive_z(0, k + 1)
+    each = local // 16 // (2 * half)
+    for n in range(2 * half):
+        build(n * each, each)
+        d, k = divmod(n, half)
+        if k > 0:
+            arrive_z(d, ks[k - 1])
+            if k + 1 == half:
+                own_far(d + 2)
 
     d0 = lax.broadcasted_iota(jnp.int32, (owners, owners), 0)
     d1 = lax.broadcasted_iota(jnp.int32, (owners, owners), 1)
@@ -156,26 +188,11 @@
     rid = lax.broadcasted_iota(jnp.int32, (rows, local), 0)
     net[...] = jnp.where(rid == row, 1.0, 0.0).astype(jnp.bfloat16)
 
-    for k in range(half):
-        arrive_y(0, k)
-    arrive_s(0)
-
-    per = 2048 // nloc
-
-    def multiply(d):
-        acc[...] = jnp.zeros_like(acc)
-
-        @pl.loop(0, owners // per)
-        def _(i):
-            cols = pl.ds(pl.multiple_of(i * (per * nloc), 128), per * nloc)
-            part = gath[d, pl.ds(i * per, per)].reshape(per * nloc, paths)
-            acc[...] += jnp.dot(weight[:, cols], part, preferred_element_type=jnp.float32)
-
-    def price():
+    def price(d):
         @pl.loop(0, local // 128)
         def _(i):
             at = pl.ds(pl.multiple_of(i * 128, 128), 128)
-            zt[...] = jnp.tanh(acc[at, :].T)
+            zt[...] = jnp.tanh(acc[d // 2, at, (d % 2) * paths:(d % 2 + 1) * paths].T)
             for p in range(paths // 32):
                 z = zt[p * 32:(p + 1) * 32, :]
                 z2 = z + z
@@ -231,22 +248,48 @@
             total = total + got3[d, k - 1]
         out[d] = jnp.maximum(total, 0.0)
 
-    for d in range(dates):
-        if d + 2 < dates:
-            own(d + 2)
-        multiply(d)
-        if d + 1 < dates:
-            for k in range(1, half):
-                arrive_z(d + 1, k)
-        price()
-        netting(d)
-        if d + 1 < dates:
-            for k in range(half):
-                arrive_y(d + 1, k)
-        stage2(d)
-        stage3(d)
-        if d + 1 < dates:
-            arrive_s(d + 1)
+    def cross(e, k):
+        arrive_y(2 * e, k)
+        arrive_y(2 * e + 1, k)
+
+    multiply(0, 0, 0)
+    cross(0, 0)
+    for n, k in enumerate(ks):
+        multiply(0, k, 0)
+        cross(0, k)
+        arrive_z(2, k)
+        multiply(0, ([0] + ks)[n], 1)
+    for k in ks:
+        arrive_z(3, k)
+    multiply(0, ks[-1], 1)
+    price(0)
+    netting(0)
+    multiply(1, 0, 0)
+    cross(1, 0)
+    stage2(0)
+    multiply(1, ks[0], 0)
+    stage3(0)
+    multiply(1, 0, 1)
+    cross(1, ks[0])
+    price(1)
+    netting(1)
+    for n in range(1, len(ks)):
+        multiply(1, ks[n], 0)
+        multiply(1, ks[n - 1], 1)
+        cross(1, ks[n])
+        if n == 1:
+            stage2(1)
+        if n == 2:
+            stage3(1)
+    multiply(1, ks[-1], 1)
+    price(2)
+    netting(2)
+    stage2(2)
+    price(3)
+    stage3(2)
+    netting(3)
+    stage2(3)
+    stage3(3)
     for d in range(dates):
         finish(d)
     for cp in pending:
@@ -269,10 +312,10 @@
         in_specs=[pl.BlockSpec(memory_space=pltpu.VMEM)] * 8,
         out_specs=pl.BlockSpec(memory_space=pltpu.VMEM),
         scratch_shapes=[
-            pltpu.VMEM((dates, owners, nloc, paths), bf16),
+            pltpu.VMEM((dates // 2, owners, 2, nloc, paths), bf16),
             pltpu.VMEM((local, owners * nloc), bf16),
             pltpu.VMEM((REFS, local, 128), f32),
-            pltpu.VMEM((local, paths), f32),
+            pltpu.VMEM((dates // 2, local, 2 * paths), f32),
             pltpu.VMEM((basis, local), f32),
             pltpu.VMEM((paths, 128), f32),
             pltpu.VMEM((2 * paths, local), bf16),

time: 116 us -> 94.6 us (0.82)
  Pallas kernels: 108 us -> 86.2 us
    pallas_call x1, Pallas kernels: 108 us -> 86.2 us  [on_device(): pl.pallas_call(functools.partial(kernel, trades), out_shape=jax.ShapeDtyp...]
where the time goes in v2:
time: 94.6 us; the launch traced here: 94.4 us
  Pallas kernels  86.2 us (91%)
  local copies, waits for them, and re-layouts  8.15 us (9%)
    pallas_call x1, Pallas kernels, on_device(): pl.pallas_call(functools.partial(kernel, trades), out_shape=jax.ShapeDtyp...  86.2 us
    unnamed x10, local copies, waits for them, and re-layouts  6.07 us

profile of v2, /device:TPU:0, one launch (start us, length us, event | category | flops | bytes accessed | tf_op | source)
XLA Modules:
  0.0 94.4 jit_solution(2831177168213127887)
XLA Ops:
  0.0 0.0 copy-start.2
  0.0 0.0 copy-start
  0.0 0.7 copy-done.2
  0.7 0.6 reshape.10.order
  1.2 1.7 %copy.10.load = bf16[1024,64]{1,0:T(8,128)(2,1)} copy(bf16[1024,64]{0,1:T(8,128)(2,1)} %param.9) | data formatting | bytes 262144 | tf_op args[1]
  3.0 1.7 %copy.11.coef = bf16[1024,64]{1,0:T(8,128)(2,1)} copy(bf16[1024,64]{0,1:T(8,128)(2,1)} %param.10) | data formatting | bytes 262144 | tf_op args[2]
  4.7 0.0 copy-done
  4.7 0.0 copy-start.1
  4.7 0.9 copy.15
  5.6 0.0 copy-done.1
  5.6 1.0 %copy.12.blocks = s32[1024,4]{1,0:T(8,128)} copy(s32[1024,4]{0,1:T(4,128)S(1)} %copy-done.1) | data formatting | bytes 32768 | tf_op args[3]
  6.6 86.2 %shard_map.82 = f32[4,32,128]{2,1,0:T(8,128)} custom-call(bf16[4,512,128]{2,1,0:T(8,128)(2,1)} %bitcast.6, bf16[1024,64]{1,0:T(8,128)(2,1)} %copy.10.load, bf16[1024,64]{1,0:T(8,128)(2,1)} %copy.11.coef, s32[1024,4]{1,0:T(8,128)} %copy.12.blocks, s32[1,1024]{1,0:T(1,128)} %bitcast.8, s32[1,384]{1,0:T(1,128)} %reshape.10.order, s32[1,16]{1,0:T(1,128)} %bitcast.9, ...), custom_call_target="tpu_custom_call" | custom-call | tf_op jit(solution)/shard_map/pallas_call | solution.py:309
  92.9 1.5 %copy.13 = f32[32,4,128]{2,1,0:T(4,128)} copy(f32[32,4,128]{2,0,1:T(8,128)} %bitcast.7) | data formatting | bytes 131072 | tf_op jit(solution)/shard_map/transpose | solution.py:344
Async XLA Ops:
  0.0 0.7 copy-start.2
  0.0 4.7 %copy-start = (bf16[512,4,128]{2,1,0:T(4,128)(2,1)S(1)}, bf16[512,4,128]{2,1,0:T(4,128)(2,1)}, u32[]{:S(2)}) copy-start(bf16[512,4,128]{2,1,0:T(4,128)(2,1)} %param.8) | copy-start | bytes 1572868
  4.7 0.9 copy-start.1
